TPU v7x, 32 devices: a whole 2x2x4 slice. The times are simulated.
32 devices in a mesh: dom: 8 (over z, y), dir: 4 (over x, core).
Axes of the slice: x: 2, y: 2, z: 4, core: 2. Of those that a mesh axis runs over, the one named last changes fastest.
Arguments:
- unknowns: bfloat16 [128, 8, 1024], P(('dom', 'dir')), may hold values from -6 to 6
- schur_blocks: bfloat16 [128, 1024, 1024], P(('dom', 'dir')), may hold values from -0.1875 to 0.1875
- adjacency: int32 [128, 4], P(('dom', 'dir')), may hold values from 0 to 127, as said below
- row_map: int32 [128, 4, 1024], P(('dom', 'dir')), may hold values from 0 to 1023
- coupling: float32 [128, 4, 1024], P(('dom', 'dir')), may hold values from -1.5 to 1.5
- owner_box: int32 [128, 256, 1], P(('dom', 'dir')), may hold values from 0 to 255; in each aligned block of 1024 rows (0 to 1023, 1024 to 2047, ..., all dimensions but the last counted through in order) at most 8 rows name the same one
- aggregation: bfloat16 [256, 256, 1152], P('dom', None, 'dir'), may hold values from -0.1875 to 0.1875
- trans_table: float32 [316, 1152], P(None, 'dir'), may hold values from -1.5 to 1.5
- inter_list: int32 [256, 16], P('dom'), may hold values from 0 to 255, as said below
- inter_type: int32 [256, 16], P('dom'), may hold values from 0 to 315
- near_list: int32 [256, 4], P(('dom', 'dir')), may hold values from 0 to 31
- near_blocks: bfloat16 [256, 4, 256, 256], P(('dom', 'dir')), may hold values from -0.375 to 0.375
Outputs:
- response: float32 [128, 8, 1024], P(('dom', 'dir'))
Inputs may be any that keep to these rules, and one draw needn't show every extreme that they name: `adjacency`: every neighbour t of subdomain s has t // 16 equal to g - 1, g or g + 1 modulo 8, with g = s // 16, and (t // 4) % 4 = (s // 4) % 4. `owner_box`: among the surface unknowns of one aligned block of 4 subdomains, no box is named more than 8 times. `inter_list`: every source box c of box b has c // 32 equal to b // 32 - 1, b // 32 or b // 32 + 1 modulo 8.
All inputs are finite; a program needn't handle non-finite values.
Results may differ from a plain program's by a relative error of at most 0.0035.
Values may be sent and summed in bfloat16 or wider, within the bound.
A program may use at most 128 MiB of HBM per device.

v0:
```python
import jax
import jax.numpy as jnp
from jax import lax
from jax.sharding import PartitionSpec as P


def padded(value, sides, width):
    for axis, dim in sides:
        count, length = (lax.axis_size(axis), value.shape[dim])
        up = [(i, (i + 1) % count) for i in range(count)]
        down = [(j, i) for i, j in up]
        last = lax.slice_in_dim(value, length - width, length, axis=dim)
        leading = lax.slice_in_dim(value, 0, width, axis=dim)
        before = lax.ppermute(last, axis, up)
        after = lax.ppermute(leading, axis, down)
        value = jnp.concatenate([before, value, after], axis=dim)
    return value


def slot_ranks(owners):
    amount = owners.shape[0]
    same = owners[:, None] == owners[None, :]
    order = jnp.arange(amount, dtype=jnp.int32)
    earlier = order[:, None] > order[None, :]
    return jnp.sum(jnp.where(same & earlier, 1, 0), axis=1).astype(jnp.int32)


def one_hot(index, width, dtype):
    return (index[..., None] == jnp.arange(width, dtype=jnp.int32)).astype(dtype)


def shards(
    unknowns,
    schur_blocks,
    adjacency,
    row_map,
    coupling,
    owner_box,
    aggregation,
    trans_table,
    inter_list,
    inter_type,
    near_list,
    near_blocks,
):
    dom_count = lax.axis_size("dom")
    dir_count = lax.axis_size("dir")
    dom_here = lax.axis_index("dom")
    sub_count, excitations, row_width = unknowns.shape
    group_boxes, box_slots, direction_count = aggregation.shape
    own_boxes, near_count = near_list.shape
    adj_count = adjacency.shape[1]
    type_count = trans_table.shape[0]
    capacity = box_slots // (dom_count * dir_count)
    surface_rows = owner_box.shape[1]
    highest = lax.Precision.HIGHEST
    schur_part = jnp.einsum(
        "sij,sej->sei", schur_blocks, unknowns, preferred_element_type=jnp.float32
    )
    window = padded(unknowns, (("dom", 0),), sub_count)
    source_dom = adjacency // (sub_count * dir_count)
    shifted = (source_dom - dom_here + 1 + dom_count) % dom_count
    local_index = shifted * sub_count + adjacency % sub_count
    chooser = one_hot(local_index, window.shape[0], jnp.bfloat16)
    picked = jnp.einsum(
        "skw,wer->sker", chooser, window, preferred_element_type=jnp.float32
    ).astype(jnp.bfloat16)
    picked_flat = picked.reshape(sub_count * adj_count, excitations, row_width)
    maps_flat = row_map.reshape(sub_count * adj_count, row_width)

    def fetch_rows(operands):
        mapping, source = operands
        selector = one_hot(mapping, row_width, jnp.bfloat16)
        return jnp.einsum("ej,ij->ei", source, selector, preferred_element_type=jnp.float32)

    fetched = lax.map(fetch_rows, (maps_flat, picked_flat)).reshape(
        sub_count, adj_count, excitations, row_width
    )
    coupled = jnp.sum(coupling[:, :, None, :] * fetched, axis=1)
    owners = owner_box[:, :, 0].reshape(-1)
    slot_rank = slot_ranks(owners)
    box_dom = owners // group_boxes
    inner_slot = owners % group_boxes * capacity + slot_rank
    destination = box_dom * (group_boxes * capacity) + inner_slot
    surface = jnp.transpose(unknowns[:, :, :surface_rows], (1, 0, 2)).reshape(excitations, -1)
    placer = one_hot(destination, dom_count * group_boxes * capacity, jnp.bfloat16)
    outgoing = jnp.dot(surface, placer, preferred_element_type=jnp.float32).astype(jnp.bfloat16)
    outgoing = outgoing.reshape(excitations, dom_count, group_boxes * capacity)
    spread = lax.all_to_all(outgoing, "dom", split_axis=1, concat_axis=1, tiled=True)
    arrived = lax.all_gather(spread[None], "dir", axis=0, tiled=True)
    group_current = arrived.reshape(dir_count, excitations, dom_count, group_boxes, capacity)
    agg_view = aggregation.reshape(group_boxes, dir_count, dom_count, capacity, direction_count)
    patterns = jnp.einsum(
        "regbc,brgcd->bed", group_current, agg_view, preferred_element_type=jnp.float32
    ).astype(jnp.bfloat16)
    nearby = padded(patterns, (("dom", 0),), group_boxes)
    source_group = inter_list // group_boxes
    position = (
        source_group - dom_here + 1 + dom_count
    ) % dom_count * group_boxes + inter_list % group_boxes
    type_hot = one_hot(inter_type, type_count, jnp.float32)
    factors = jnp.einsum("hjt,td->hjd", type_hot, trans_table, precision=highest)
    place_hot = one_hot(position, nearby.shape[0], jnp.float32)
    weights = jnp.einsum("hjw,hjd->hwd", place_hot, factors, precision=highest)
    incoming = jnp.einsum(
        "hwd,wed->hed", weights, nearby.astype(jnp.float32), precision=highest
    ).astype(jnp.bfloat16)
    partial_term = jnp.einsum(
        "hpd,hed->hep", aggregation, incoming, preferred_element_type=jnp.float32
    ).astype(jnp.bfloat16)
    partial_term = lax.optimization_barrier(partial_term)
    far_field = lax.psum_scatter(
        partial_term.astype(jnp.float32).astype(jnp.bfloat16),
        "dir",
        scatter_dimension=0,
        tiled=True,
    ).astype(jnp.float32)
    near_hot = one_hot(near_list, group_boxes, jnp.bfloat16)
    near_sources = jnp.einsum(
        "hjb,regbc->reghjc", near_hot, group_current, preferred_element_type=jnp.float32
    ).astype(jnp.bfloat16)
    near_view = near_blocks.reshape(
        own_boxes, near_count, box_slots, dir_count, dom_count, capacity
    )
    near_field = jnp.einsum(
        "reghjc,hjprgc->hep", near_sources, near_view, preferred_element_type=jnp.float32
    )
    box_fields = (far_field + near_field).astype(jnp.bfloat16)
    leaving = box_fields.reshape(own_boxes, excitations, dir_count, dom_count, capacity)
    returned = lax.all_to_all(
        lax.all_to_all(leaving, "dom", split_axis=3, concat_axis=0, tiled=True),
        "dir",
        split_axis=2,
        concat_axis=0,
        tiled=True,
    )
    returned = jnp.transpose(
        returned.reshape(dir_count * dom_count * own_boxes, excitations, capacity), (0, 2, 1)
    )
    returned = returned.reshape(-1, excitations)
    box_within = owners % group_boxes
    position_back = (
        box_within // own_boxes * dom_count + box_dom
    ) * own_boxes + box_within % own_boxes
    taker = one_hot(position_back * capacity + slot_rank, returned.shape[0], jnp.bfloat16)
    surface_field = jnp.dot(taker, returned, preferred_element_type=jnp.float32)
    surface_field = jnp.transpose(
        surface_field.reshape(sub_count, surface_rows, excitations), (0, 2, 1)
    )
    combined = schur_part + coupled
    return combined.at[:, :, :surface_rows].add(surface_field)


def solution(mesh):
    in_specs = (
        P(("dom", "dir"), None, None),
        P(("dom", "dir"), None, None),
        P(("dom", "dir"), None),
        P(("dom", "dir"), None, None),
        P(("dom", "dir"), None, None),
        P(("dom", "dir"), None, None),
        P("dom", None, "dir"),
        P(None, "dir"),
        P("dom", None),
        P("dom", None),
        P(("dom", "dir"), None),
        P(("dom", "dir"), None, None, None),
    )
    out_specs = P(("dom", "dir"), None, None)
    return jax.shard_map(shards, mesh=mesh, in_specs=in_specs, out_specs=out_specs, check_vma=False)
```

profile of v0, /device:TPU:0, one launch (start us, length us, event | category | flops | bytes accessed | tf_op | source)
XLA Modules:
  0.0 156.8 jit_solution(2086558005152994952)
XLA Ops:
  6.5 0.9 copy.98
  7.5 3.0 %collective-permute-start = (bf16[4,8,1024]{2,0,1:T(4,128)(2,1)S(1)}, bf16[4,8,1024]{2,0,1:T(4,128)(2,1)S(1)}, u32[]{:S(2)}, u32[]{:S(2)}) collective-permute-start(bf16[4,8,1024]{2,0,1:T(4,128)(2,1)S(1)} %copy.98), channel_id=1, source_target_pairs={{0,4},{4,8},{8,12},{12,16},{16,20},{20,24},{24,28},{28,0},{1,5},{5... | collective-permute-start | bytes 196616 | tf_op jit(solution)/shard_map/ppermute | solution.py:14
  10.5 3.1 %collective-permute-start.1 = (bf16[4,8,1024]{2,0,1:T(4,128)(2,1)S(1)}, bf16[4,8,1024]{2,0,1:T(4,128)(2,1)S(1)}, u32[]{:S(2)}, u32[]{:S(2)}) collective-permute-start(bf16[4,8,1024]{2,0,1:T(4,128)(2,1)S(1)} %copy.98), channel_id=1, source_target_pairs={{4,0},{8,4},{12,8},{16,12},{20,16},{24,20},{28,24},{0,28},{5,1},{9... | collective-permute-start | bytes 196616 | tf_op jit(solution)/shard_map/ppermute | solution.py:15
  14.3 1.4 select_reduce_fusion
  16.4 2.1 %fusion.18 = bf16[2048,8]{0,1:T(8,128)(2,1)} fusion(bf16[8,1024]{1,0:T(8,128)(2,1)S(1)} %bitcast.139, s32[1024]{0:T(1024)S(1)} %fusion.87), kind=kOutput, calls=%fused_computation.23 | convolution fusion | flops 35667968 | bytes 53248 | tf_op jit(solution)/shard_map/dot_general | solution.py:87
  18.5 3.5 %all-to-all-start = ((bf16[8,8,256]{2,0,1:T(8,128)(2,1)}), bf16[8,8,256]{2,0,1:T(8,128)(2,1)S(1)}, u32[]{:S(2)}, u32[]{:S(2)}) async-start(bf16[8,8,256]{2,0,1:T(8,128)(2,1)} %bitcast.13), calls=%async_computation | async-start | bytes 65536 | tf_op jit(solution)/shard_map/all_to_all | solution.py:89
  22.0 0.7 fusion.75
  22.8 0.8 copy.107
  24.3 1.0 fusion.60
  25.3 4.1 %fusion.67 = f32[32,96,288]{2,1,0:T(8,128)} fusion(f32[32,16,288]{2,1,0:T(8,128)S(1)} %fusion.60, s32[32,16]{1,0:T(8,128)S(1)} %copy.106), kind=kOutput, calls=%fused_computation.54 | convolution fusion | flops 169918464 | bytes 4130816 | tf_op jit(solution)/shard_map/hjw,hjd->hwd/dot_general | solution.py:104
  29.5 8.0 %copy.103 = bf16[32,256,288]{2,1,0:T(8,128)(2,1)} copy(bf16[32,256,288]{1,2,0:T(8,128)(2,1)} %param.22) | data formatting | bytes 9437184 | tf_op args[6]
  37.4 5.9 %copy.109 = f32[32,96,288]{1,0,2:T(8,128)} copy(f32[32,96,288]{2,1,0:T(8,128)} %fusion.67) | data formatting | bytes 7077888 | tf_op jit(solution)/shard_map/hjw,hjd->hwd/dot_general | solution.py:104
  43.4 6.5 %copy.113 = bf16[8,4,256,256]{2,3,1,0:T(8,128)(2,1)} copy(bf16[8,4,256,256]{3,2,1,0:T(8,128)(2,1)} %param.27) | data formatting | bytes 8388608 | tf_op args[11]
  50.5 5.4 %all-gather = bf16[32,8,256]{2,1,0:T(8,128)(2,1)S(1)} all-gather(bf16[8,8,256]{2,1,0:T(8,128)(2,1)S(1)} %copy.102), channel_id=2, replica_groups=mesh['dom'=8,'dir'=4] {'dir'}, dimensions={0}, use_global_device_ids=true | all-gather | bytes 163840 | tf_op jit(solution)/shard_map/all_gather | solution.py:90
  56.0 2.5 %reshape.208 = bf16[4,8,8,32,8]{4,3,2,1,0:T(8,128)(2,1)S(1)} reshape(bf16[32,8,256]{2,1,0:T(8,128)(2,1)S(1)} %all-gather) | data formatting | bytes 262144 | tf_op jit(solution)/shard_map/reshape | solution.py:91
  58.4 6.5 %fusion.31 = bf16[32,8,288]{2,1,0:T(8,128)(2,1)S(1)} fusion(bf16[32,4,8,8,288]{4,3,2,1,0:T(8,128)(2,1)} %bitcast.130, bf16[4,8,8,32,8]{4,3,2,1,0:T(8,128)(2,1)S(1)} %reshape.208), kind=kOutput, calls=%fused_computation.33 | convolution fusion | flops 37822464 | bytes 4997120 | tf_op jit(solution)/shard_map/regbc,brgcd->bed/dot_general | solution.py:93
  64.9 1.9 %collective-permute-start.2 = (bf16[32,8,288]{2,1,0:T(8,128)(2,1)S(1)}, bf16[32,8,288]{2,1,0:T(8,128)(2,1)S(1)}, u32[]{:S(2)}, u32[]{:S(2)}) collective-permute-start(bf16[32,8,288]{2,1,0:T(8,128)(2,1)S(1)} %fusion.31), channel_id=1, source_target_pairs={{0,4},{4,8},{8,12},{12,16},{16,20},{20,24},{24,28},{28,0},{1,5},{5... | collective-permute-start | bytes 442376 | tf_op jit(solution)/shard_map/ppermute | solution.py:14
  66.8 2.9 %collective-permute-start.3 = (bf16[32,8,288]{2,1,0:T(8,128)(2,1)S(1)}, bf16[32,8,288]{2,1,0:T(8,128)(2,1)S(1)}, u32[]{:S(2)}, u32[]{:S(2)}) collective-permute-start(bf16[32,8,288]{2,1,0:T(8,128)(2,1)S(1)} %fusion.31), channel_id=1, source_target_pairs={{4,0},{8,4},{12,8},{16,12},{20,16},{24,20},{28,24},{0,28},{5,1},{9... | collective-permute-start | bytes 442376 | tf_op jit(solution)/shard_map/ppermute | solution.py:15
  69.7 2.6 %convert_bitcast_fusion = bf16[4,8,8,8,4,8]{5,4,3,2,1,0:T(4,128)(2,1)} fusion(bf16[4,8,8,32,8]{4,3,2,1,0:T(8,128)(2,1)S(1)} %reshape.208, s32[8,4]{1,0:T(8,128)S(1)} %copy.111), kind=kOutput, calls=%fused_computation.28 | convolution fusion | flops 4260864 | bytes 262272 | tf_op jit(solution)/shard_map/hjb,regbc->reghjc/dot_general | solution.py:119
  72.7 2.9 %collective-permute-done.2 = bf16[32,8,288]{2,1,0:T(8,128)(2,1)S(1)} collective-permute-done((bf16[32,8,288]{2,1,0:T(8,128)(2,1)S(1)}, bf16[32,8,288]{2,1,0:T(8,128)(2,1)S(1)}, u32[]{:S(2)}, u32[]{:S(2)}) %collective-permute-start.2) | collective-permute-done | bytes 147488 | tf_op jit(solution)/shard_map/ppermute | solution.py:14
  75.6 2.2 %collective-permute-done.3 = bf16[32,8,288]{2,1,0:T(8,128)(2,1)S(1)} collective-permute-done((bf16[32,8,288]{2,1,0:T(8,128)(2,1)S(1)}, bf16[32,8,288]{2,1,0:T(8,128)(2,1)S(1)}, u32[]{:S(2)}, u32[]{:S(2)}) %collective-permute-start.3) | collective-permute-done | bytes 147488 | tf_op jit(solution)/shard_map/ppermute | solution.py:15
  78.5 6.1 %fusion.25 = bf16[32,8,288]{0,1,2:T(8,128)(2,1)S(1)} fusion(bf16[96,8,288]{0,1,2:T(8,128)(2,1)S(1)} %copy.108, f32[32,96,288]{1,0,2:T(8,128)} %copy.109), kind=kOutput, calls=%fused_computation.30 | convolution fusion | flops 85008384 | bytes 4128768 | tf_op jit(solution)/shard_map/hwd,wed->hed/dot_general | solution.py:105
  85.1 3.9 %convolution_convert_fusion.2 = bf16[32,8,256]{2,1,0:T(8,128)(2,1)} fusion(bf16[32,8,288]{2,1,0:T(8,128)(2,1)S(1)} %copy.110, bf16[32,256,288]{1,2,0:T(8,128)(2,1)} %param.22), kind=kOutput, calls=%fused_computation.34 | convolution fusion | flops 37814272 | bytes 4997120 | tf_op jit(solution)/shard_map/hpd,hed->hep/dot_general | solution.py:108
  89.0 26.5 %while.11 = (s32[]{:T(128)}, f32[16,8,1024]{2,1,0:T(8,128)S(1)}, bf16[16,8,1024]{2,1,0:T(8,128)(2,1)S(1)}, s32[16,1024]{1,0:T(8,128)}, s32[]{:T(128)}) while((s32[]{:T(128)}, f32[16,8,1024]{2,1,0:T(8,128)S(1)}, bf16[16,8,1024]{2,1,0:T(8,128)(2,1)S(1)}, s32[16,1024]{1,0:T(8,128)}, s32[]{:T(128)}) %tuple.27), condition=%wide.region_1.2_spmd, body=%wide.region_0.1_spmd.sunk | while | flops 17825792 | bytes 62529 | solution.py:76
  89.1 0.8 constant_dynamic-slice_fusion.2
  89.8 0.9 fusion.120
  90.7 0.8 constant_dynamic-slice_fusion.2
  91.5 0.9 fusion.120
  92.4 0.8 constant_dynamic-slice_fusion.2
  93.1 0.9 fusion.120
  94.0 0.8 constant_dynamic-slice_fusion.2
  94.8 0.9 fusion.120
  95.7 0.8 constant_dynamic-slice_fusion.2
  96.5 0.9 fusion.120
  97.4 0.8 constant_dynamic-slice_fusion.2
  98.1 0.9 fusion.120
  99.0 0.8 constant_dynamic-slice_fusion.2
  99.8 0.9 fusion.120
  100.7 0.8 constant_dynamic-slice_fusion.2
  101.4 0.9 fusion.120
  102.3 0.8 constant_dynamic-slice_fusion.2
  103.1 0.9 fusion.120
  104.0 0.8 constant_dynamic-slice_fusion.2
  104.8 0.9 fusion.120
  105.6 0.8 constant_dynamic-slice_fusion.2
  106.4 0.9 fusion.120
  107.3 0.8 constant_dynamic-slice_fusion.2
  108.1 0.9 fusion.120
  109.0 0.8 constant_dynamic-slice_fusion.2
  109.7 0.9 fusion.120
  110.6 0.8 constant_dynamic-slice_fusion.2
  111.4 0.9 fusion.120
  112.3 0.8 constant_dynamic-slice_fusion.2
  113.0 0.9 fusion.120
  113.9 0.8 constant_dynamic-slice_fusion.2
  114.7 0.9 fusion.120
  115.6 4.7 %fusion.46 = bf16[8,8,256]{2,1,0:T(8,128)(2,1)S(1)} fusion(bf16[8,4,256,4,8,8]{2,5,4,3,1,0:T(8,128)(2,1)} %bitcast.131, bf16[4,8,8,8,4,8]{5,4,3,2,1,0:T(4,128)(2,1)S(1)} %copy-done.1, bf16[8,8,256]{2,1,0:T(8,128)(2,1)} %reduce-scatter.2.cloned.1.call-done), kind=kOutput, calls=%fused_computation.38 | convolution fusion | flops 33603584 | bytes 4390912 | tf_op jit(solution)/shard_map/reghjc,hjprgc->hep/dot_general | solution.py:125
  121.6 1.1 reshape.226
  122.7 4.3 %all-to-all-start.1 = ((bf16[8,2,1024]{2,1,0:T(2,128)(2,1)}), bf16[8,2,1024]{2,1,0:T(2,128)(2,1)S(1)}, u32[]{:S(2)}, u32[]{:S(2)}) async-start(bf16[8,2,1024]{2,1,0:T(2,128)(2,1)} %reshape.226), calls=%async_computation.2 | async-start | bytes 65536 | tf_op jit(solution)/shard_map/all_to_all | solution.py:131
  127.1 6.6 %all-to-all-done.1 = bf16[8,2,1024]{2,1,0:T(2,128)(2,1)S(1)} async-done(((bf16[8,2,1024]{2,1,0:T(2,128)(2,1)}), bf16[8,2,1024]{2,1,0:T(2,128)(2,1)S(1)}, u32[]{:S(2)}, u32[]{:S(2)}) %all-to-all-start.1) | async-done | bytes 32800 | tf_op jit(solution)/shard_map/all_to_all | solution.py:131
  135.3 0.7 reshape.228
  136.0 3.3 %all-to-all-start.2 = ((bf16[4,2,2048]{2,1,0:T(2,128)(2,1)}), bf16[4,2,2048]{2,1,0:T(2,128)(2,1)S(1)}, u32[]{:S(2)}, u32[]{:S(2)}) async-start(bf16[4,2,2048]{2,1,0:T(2,128)(2,1)} %reshape.228), calls=%async_computation.3 | async-start | bytes 65536 | tf_op jit(solution)/shard_map/all_to_all | solution.py:130
  139.3 6.3 %convolution_add_fusion = f32[4,8,1024]{2,1,0:T(8,128)} fusion(f32[4,8,1024]{2,1,0:T(8,128)S(1)} %multiply_reduce_fusion, bf16[4,8,1024]{2,1,0:T(8,128)(2,1)S(1)} %copy-done.2, bf16[4,1024,1024]{2,1,0:T(8,128)(2,1)} %param.17), kind=kOutput, calls=%fused_computation.35 | convolution fusion | flops 67141632 | bytes 8716288 | tf_op jit(solution)/shard_map/sij,sej->sei/dot_general | solution.py:57
  146.9 3.0 %fusion.57 = f32[4,8,1024]{2,1,0:T(8,128)} fusion(f32[4,8,1024]{2,1,0:T(8,128)} %convolution_add_fusion, bf16[2048,8,1]{0,1,2:T(8,128)(2,1)S(1)} %reshape.223, s32[4,256]{1,0:T(4,128)S(1)} %fusion.85), kind=kOutput, calls=%fused_computation.41 | convolution fusion | flops 35659776 | bytes 102400 | tf_op jit(solution)/shard_map/dot_general | solution.py:146
  (49 shorter events, 8.8 us)
Async XLA Ops:
  6.5 17.8 %copy-start = (f32[316,288]{0,1:T(8,128)S(1)}, f32[316,288]{0,1:T(8,128)}, u32[]{:S(2)}) copy-start(f32[316,288]{0,1:T(8,128)} %param.23) | copy-start | bytes 1092100
  7.5 64.8 %collective-permute-start = (bf16[4,8,1024]{2,0,1:T(4,128)(2,1)S(1)}, bf16[4,8,1024]{2,0,1:T(4,128)(2,1)S(1)}, u32[]{:S(2)}, u32[]{:S(2)}) collective-permute-start(bf16[4,8,1024]{2,0,1:T(4,128)(2,1)S(1)} %copy.98), channel_id=1, source_target_pairs={{0,4},{4,8},{8,12},{12,16},{16,20},{20,24},{24,28},{28,0},{1,5},{5... | collective-permute-start | bytes 196616 | tf_op jit(solution)/shard_map/ppermute | solution.py:14
  10.5 61.8 %collective-permute-start.1 = (bf16[4,8,1024]{2,0,1:T(4,128)(2,1)S(1)}, bf16[4,8,1024]{2,0,1:T(4,128)(2,1)S(1)}, u32[]{:S(2)}, u32[]{:S(2)}) collective-permute-start(bf16[4,8,1024]{2,0,1:T(4,128)(2,1)S(1)} %copy.98), channel_id=1, source_target_pairs={{4,0},{8,4},{12,8},{16,12},{20,16},{24,20},{28,24},{0,28},{5,1},{9... | collective-permute-start | bytes 196616 | tf_op jit(solution)/shard_map/ppermute | solution.py:15
  18.5 10.9 %copy-start.6 = (s32[4,4]{1,0:T(4,128)S(1)}, s32[4,4]{1,0:T(4,128)}, u32[]{:S(2)}) copy-start(s32[4,4]{1,0:T(4,128)} %param.18) | copy-start | bytes 196
  18.5 32.0 %all-to-all-start = ((bf16[8,8,256]{2,0,1:T(8,128)(2,1)}), bf16[8,8,256]{2,0,1:T(8,128)(2,1)S(1)}, u32[]{:S(2)}, u32[]{:S(2)}) async-start(bf16[8,8,256]{2,0,1:T(8,128)(2,1)} %bitcast.13), calls=%async_computation | async-start | bytes 65536 | tf_op jit(solution)/shard_map/all_to_all | solution.py:89
  22.0 93.6 %reduce-scatter.2.cloned.1.call-start = ((), (), s32[]{:S(2)}) async-start(), calls=%async_computation.4 | async-start | bytes 163840 | tf_op jit(solution)/shard_map/reduce_scatter | solution.py:112
  37.4 5.9 %copy-start.5 = (s32[8,4]{0,1:T(4,128)S(1)}, s32[8,4]{0,1:T(4,128)}, u32[]{:S(2)}) copy-start(s32[8,4]{0,1:T(4,128)} %param.26) | copy-start | bytes 388
  43.4 6.5 %copy-start.3 = (s32[4,4,1024]{2,1,0:T(4,128)S(1)}, s32[4,4,1024]{2,1,0:T(4,128)}, u32[]{:S(2)}) copy-start(s32[4,4,1024]{2,1,0:T(4,128)} %param.19) | copy-start | bytes 196612
  64.9 10.8 %collective-permute-start.2 = (bf16[32,8,288]{2,1,0:T(8,128)(2,1)S(1)}, bf16[32,8,288]{2,1,0:T(8,128)(2,1)S(1)}, u32[]{:S(2)}, u32[]{:S(2)}) collective-permute-start(bf16[32,8,288]{2,1,0:T(8,128)(2,1)S(1)} %fusion.31), channel_id=1, source_target_pairs={{0,4},{4,8},{8,12},{12,16},{16,20},{20,24},{24,28},{28,0},{1,5},{5... | collective-permute-start | bytes 442376 | tf_op jit(solution)/shard_map/ppermute | solution.py:14
  66.8 11.1 %collective-permute-start.3 = (bf16[32,8,288]{2,1,0:T(8,128)(2,1)S(1)}, bf16[32,8,288]{2,1,0:T(8,128)(2,1)S(1)}, u32[]{:S(2)}, u32[]{:S(2)}) collective-permute-start(bf16[32,8,288]{2,1,0:T(8,128)(2,1)S(1)} %fusion.31), channel_id=1, source_target_pairs={{4,0},{8,4},{12,8},{16,12},{20,16},{24,20},{28,24},{0,28},{5,1},{9... | collective-permute-start | bytes 442376 | tf_op jit(solution)/shard_map/ppermute | solution.py:15
  85.1 30.5 %copy-start.1 = (bf16[4,8,8,8,4,8]{5,4,3,2,1,0:T(4,128)(2,1)S(1)}, bf16[4,8,8,8,4,8]{5,4,3,2,1,0:T(4,128)(2,1)}, u32[]{:S(2)}) copy-start(bf16[4,8,8,8,4,8]{5,4,3,2,1,0:T(4,128)(2,1)} %convert_bitcast_fusion) | copy-start | bytes 393220
  115.6 11.4 %copy-start.4 = (f32[4,4,1024]{2,1,0:T(4,128)S(1)}, f32[4,4,1024]{2,1,0:T(4,128)}, u32[]{:S(2)}) copy-start(f32[4,4,1024]{2,1,0:T(4,128)} %param.20) | copy-start | bytes 196612
  120.3 19.0 %copy-start.2 = (bf16[4,8,1024]{2,1,0:T(8,128)(2,1)S(1)}, bf16[4,8,1024]{2,1,0:T(8,128)(2,1)}, u32[]{:S(2)}) copy-start(bf16[4,8,1024]{2,1,0:T(8,128)(2,1)} %param.16) | copy-start | bytes 196612
  122.7 11.0 %all-to-all-start.1 = ((bf16[8,2,1024]{2,1,0:T(2,128)(2,1)}), bf16[8,2,1024]{2,1,0:T(2,128)(2,1)S(1)}, u32[]{:S(2)}, u32[]{:S(2)}) async-start(bf16[8,2,1024]{2,1,0:T(2,128)(2,1)} %reshape.226), calls=%async_computation.2 | async-start | bytes 65536 | tf_op jit(solution)/shard_map/all_to_all | solution.py:131
  136.0 9.6 %all-to-all-start.2 = ((bf16[4,2,2048]{2,1,0:T(2,128)(2,1)}), bf16[4,2,2048]{2,1,0:T(2,128)(2,1)S(1)}, u32[]{:S(2)}, u32[]{:S(2)}) async-start(bf16[4,2,2048]{2,1,0:T(2,128)(2,1)} %reshape.228), calls=%async_computation.3 | async-start | bytes 65536 | tf_op jit(solution)/shard_map/all_to_all | solution.py:130
Sparse Core Ops, SparseCore 0:
  89.2 19.4 reduce-scatter.1
where the time goes:
time: 159 us; the launch traced here: 157 us
  matrix products  54.7 us (34%)
  local copies, waits for them, and re-layouts  45.5 us (29%)
  starting transfers between devices  22 us (14%)
  between operations  13.6 us (9%)
  waiting for transfers between devices  11.8 us (7%)
  blocking collectives  5.43 us (3%)
  other arithmetic  3.71 us (2%)
    unnamed x23, local copies, waits for them, and re-layouts  18.8 us
    dot_general x16, matrix products, fetch_rows(): jnp.einsum('ej,ij->ei', source, selector, preferred_element_type=jnp.floa...  14.2 us
    dynamic_slice x16, local copies, waits for them, and re-layouts, shards(): lax.map(fetch_rows, (maps_flat, picked_flat))  12.3 us
    all_to_all x1, waiting for transfers between devices, shards(): lax.all_to_all(leaving, 'dom', split_axis=3, concat_axis=0, tiled=True)  6.61 us
    dot_general x1, matrix products, shards(): jnp.einsum('regbc,brgcd->bed', group_current, agg_view, preferred_element...  6.45 us
    dot_general x1, matrix products, shards(): jnp.einsum('sij,sej->sei', schur_blocks, unknowns, preferred_element_type...  6.32 us
    dot_general x1, matrix products, shards(): jnp.einsum('hwd,wed->hed', weights, nearby.astype(jnp.float32), precision...  6.1 us
    ppermute x2, starting transfers between devices, padded(): after = lax.ppermute(leading, axis, down)  6.03 us
  transfers between devices with their start and end apart: 8, of which 3 were waited for; matrix products, arithmetic and copies ran while one was open for 50% of the time, Pallas kernels for 0%

commit v1 on v0

v1 whole, which is shorter than its diff:
```python
import functools

import jax
import jax.numpy as jnp
from jax import lax
from jax.experimental import pallas as pl
from jax.experimental.pallas import tpu as pltpu
from jax.sharding import PartitionSpec as P

MESH = pl.DeviceIdType.MESH
LANES = 128
F32 = jnp.float32
BF16 = jnp.bfloat16


def dot(a, b, ca, cb):
    return lax.dot_general(a, b, (((ca,), (cb,)), ((), ())), preferred_element_type=F32)


def iota(shape, dim):
    return lax.broadcasted_iota(jnp.int32, shape, dim)


def shift_of(value):
    bits = value.bit_length() - 1
    assert value == 1 << bits
    return bits


def kernel(
    dims,
    adj_ref,
    list_ref,
    type_ref,
    near_ref,
    unk_ref,
    owner_ref,
    agg_hbm,
    trans_hbm,
    maps_hbm,
    coup_hbm,
    schur_hbm,
    blocks_hbm,
    out_ref,
    agg_v,
    trans_v,
    trans_t,
    maps_v,
    coup_v,
    schur_v,
    blocks_v,
    place,
    perm,
    send1,
    recv1,
    recv0,
    winf,
    curf,
    pats,
    recv2,
    patf,
    coupled,
    nearf,
    total,
    send3,
    recv3,
    local_sem,
    schur_sem,
    send_sem,
    recv_sem,
    side_send,
    side_recv,
    wide_send,
    wide_recv,
):
    doms, dirs = dims
    devices = doms * dirs
    subs, excites, rows = unk_ref.shape
    boxes, directions, slots = agg_v.shape
    near_count, own = near_ref.shape
    adj_count = adj_ref.shape[1]
    list_len = list_ref.shape[0]
    surface = owner_ref.shape[1] // subs
    capacity = slots // devices
    per_tile = LANES // excites
    halves = boxes // per_tile
    unit = max(16, halves * capacity)
    amount = subs * surface
    all_rows = devices * unit
    my_dom = lax.axis_index("dom")
    my_dir = lax.axis_index("dir")
    me = my_dom * dirs + my_dir
    my_slot = my_dir * doms + my_dom
    right, left = lax.rem(my_dom + 1, doms), lax.rem(my_dom + doms - 1, doms)

    barrier = pltpu.get_barrier_semaphore()

    def greet(k, carry):
        other = lax.rem(me + k, devices)
        pl.semaphore_signal(
            barrier,
            inc=1,
            device_id=(lax.div(other, dirs), lax.rem(other, dirs)),
            device_id_type=MESH,
        )
        return carry

    lax.fori_loop(1, devices, greet, 0)

    locals_ = [
        pltpu.make_async_copy(src, dst, local_sem.at[i])
        for i, (src, dst) in enumerate(
            [
                (agg_hbm, agg_v),
                (trans_hbm, trans_t),
                (maps_hbm, maps_v),
                (coup_hbm, coup_v),
                (blocks_hbm, blocks_v),
            ]
        )
    ]
    schurs = [
        pltpu.make_async_copy(schur_hbm.at[s], schur_v.at[s], schur_sem.at[s]) for s in range(subs)
    ]
    locals_[0].start()
    schurs[0].start()
    schurs[1].start()
    locals_[4].start()
    for i in (1, 2, 3):
        locals_[i].start()
    for s in range(2, subs):
        schurs[s].start()

    owner_row = owner_ref[...]
    owner_col = jnp.concatenate(
        [
            jnp.broadcast_to(owner_row[:, k : k + LANES], (LANES, LANES)).T
            for k in range(0, amount, LANES)
        ],
        axis=0,
    )
    order = iota((amount, LANES), 0)
    ahead = order - iota((amount, LANES), 1)
    ranks = []
    for k in range(0, amount, LANES):
        same = (owner_col == owner_row[:, k : k + LANES]) & (ahead < k)
        ranks.append(jnp.sum(jnp.where(same, 1.0, 0.0), axis=0, keepdims=True))
    rank = jnp.concatenate(ranks, axis=1).astype(jnp.int32)
    half = (owner_row & (boxes - 1)) >> shift_of(per_tile)
    key = (owner_row >> shift_of(boxes)) * unit + half * capacity + rank
    place[...] = jnp.where(iota((doms * unit, amount), 0) == key, 1.0, 0.0).astype(BF16)
    wide = []
    for s in range(subs):
        piece = unk_ref[s][:, :surface].astype(F32)
        wide.append(jnp.concatenate([piece] * per_tile, axis=0).T)
    wide = jnp.concatenate(wide, axis=0)
    lane_box = iota((amount, LANES), 1) >> shift_of(excites)
    wide = jnp.where((owner_col & (per_tile - 1)) == lane_box, wide, 0.0).astype(BF16)
    send1[...] = dot(place[...], wide, 1, 0).astype(BF16)

    row = iota((all_rows, slots), 0)
    col = iota((all_rows, slots), 1)
    within = row & (unit - 1)
    slot_of = (row >> shift_of(unit)) * capacity + (within & (capacity - 1))
    for h in range(halves):
        hit = (slot_of == col) & ((within >> shift_of(capacity)) == h)
        perm[h] = jnp.where(hit, 1.0, 0.0).astype(BF16)

    pl.semaphore_wait(barrier, devices - 1)

    def tile(index):
        return pl.ds(pl.multiple_of(index * unit, unit), unit)

    def scatter(k, carry):
        other = lax.rem(me + k, devices)
        to_dom, to_dir = lax.div(other, dirs), lax.rem(other, dirs)
        pltpu.make_async_remote_copy(
            src_ref=send1.at[tile(to_dom)],
            dst_ref=recv1.at[tile(my_slot)],
            send_sem=send_sem.at[0],
            recv_sem=recv_sem.at[0],
            device_id=(to_dom, to_dir),
            device_id_type=MESH,
        ).start()
        return carry

    lax.fori_loop(1, devices, scatter, 0)
    recv1[tile(my_slot), :] = send1[tile(my_dom), :]

    sides = []
    for side, target in enumerate((right, left)):
        copy = pltpu.make_async_remote_copy(
            src_ref=unk_ref,
            dst_ref=recv0.at[side],
            send_sem=side_send.at[side],
            recv_sem=side_recv.at[side],
            device_id=(target, my_dir),
            device_id_type=MESH,
        )
        copy.start()
        sides.append(copy)

    block = 256

    def schur(s):
        schurs[s].wait()
        unknown = unk_ref[s]

        def part(i, carry):
            at = pl.ds(pl.multiple_of(i * block, block), block)
            out_ref[s, :, at] = dot(unknown, schur_v[s, at, :], 1, 1)
            return carry

        lax.fori_loop(0, rows // block, part, 0)

    schur(0)
    schur(1)

    def drain(buffer, sem):
        size = pl.ds(0, all_rows - unit)
        pltpu.make_async_copy(buffer.at[size], buffer.at[size], sem).wait()

    drain(recv1, recv_sem.at[0])
    arrived = recv1[...]
    for h in range(halves):
        piece = dot(arrived, perm[h], 0, 0)
        curf[h * per_tile : (h + 1) * per_tile] = piece.reshape(per_tile, excites, slots)

    locals_[0].wait()
    chunks = 4
    chunk_boxes = boxes // chunks
    pair = 2
    wides = []
    for c in range(chunks):

        def radiate(i, carry):
            first = c * chunk_boxes + i * pair
            found = []
            for k in range(pair):
                b = first + k
                found.append(dot(curf[b].astype(BF16), agg_v[b], 1, 1))
            both = jnp.concatenate(found, axis=0).astype(BF16)
            pats[pl.ds(pl.multiple_of(first * excites, 16), 16), :] = both
            patf[pl.ds(boxes + first, pair)] = both.astype(F32).reshape(pair, excites, directions)
            return carry

        lax.fori_loop(0, chunk_boxes // pair, radiate, 0)
        at = pl.ds(c * chunk_boxes * excites, chunk_boxes * excites)
        for side, target in enumerate((right, left)):
            copy = pltpu.make_async_remote_copy(
                src_ref=pats.at[at],
                dst_ref=recv2.at[side, at],
                send_sem=wide_send.at[side, c],
                recv_sem=wide_recv.at[side, c],
                device_id=(target, my_dir),
                device_id_type=MESH,
            )
            copy.start()
            wides.append(copy)

    locals_[1].wait()
    trans_v[...] = trans_t[...].T

    locals_[4].wait()
    nearf[...] = jnp.zeros_like(nearf)

    def near(b, carry):
        field = jnp.zeros((excites, slots), F32)
        for j in range(near_count):
            source = curf[near_ref[j, b]].astype(BF16)
            field = field + dot(source, blocks_v[b, j], 1, 1)
        nearf[my_dir * own + b] = field
        return carry

    lax.fori_loop(0, own, near, 0)

    for copy in sides:
        copy.wait_recv()
    winf[0:subs] = recv0[0].astype(F32)
    winf[subs : 2 * subs] = unk_ref[...].astype(F32)
    winf[2 * subs : 3 * subs] = recv0[1].astype(F32)
    locals_[2].wait()
    locals_[3].wait()
    group_subs = subs * dirs
    sub_base = left * group_subs

    def couple(s, carry):
        fields = [jnp.zeros((excites, LANES), F32)] * (rows // LANES)
        for k in range(adj_count):
            offset = adj_ref[s, k] - sub_base
            offset = jnp.where(offset < 0, offset + group_subs * doms, offset)
            offset = jnp.minimum(offset, 3 * group_subs - 1)
            source = winf[lax.div(offset, group_subs) * subs + lax.rem(offset, subs)]
            mapping = maps_v[s, k : k + 1, :]
            factor = coup_v[s, k : k + 1, :]
            for c in range(rows // LANES):
                at = slice(c * LANES, (c + 1) * LANES)
                index = jnp.broadcast_to(mapping[:, at], (excites, LANES))
                low, high = index & (LANES - 1), index >> shift_of(LANES)
                value = jnp.zeros((excites, LANES), F32)
                for q in range(rows // LANES):
                    got = jnp.take_along_axis(
                        source[:, q * LANES : (q + 1) * LANES],
                        low,
                        axis=1,
                        mode="promise_in_bounds",
                    )
                    value = jnp.where(high == q, got, value)
                fields[c] = fields[c] + factor[:, at] * value
        coupled[s] = jnp.concatenate(fields, axis=1)
        return carry

    lax.fori_loop(0, subs, couple, 0)
    for s in range(2, subs - 1):
        schur(s)

    for copy in wides:
        copy.wait_recv()
    for side, base in ((0, 0), (1, 2 * boxes)):
        patf[base : base + boxes] = recv2[side].astype(F32).reshape(boxes, excites, directions)

    box_base = left * boxes

    def respond(i, carry):
        first = i * pair
        found = []
        for k in range(pair):
            b = first + k
            field = jnp.zeros((excites, directions), F32)
            for j in range(list_len):
                offset = list_ref[j, b] - box_base
                offset = jnp.where(offset < 0, offset + boxes * doms, offset)
                offset = jnp.minimum(offset, 3 * boxes - 1)
                field = field + trans_v[pl.ds(type_ref[j, b], 1), :] * patf[offset]
            found.append(dot(field.astype(BF16), agg_v[b], 1, 0) + nearf[b])
        both = jnp.concatenate(found, axis=0).astype(BF16)
        total[pl.ds(pl.multiple_of(first * excites, 16), 16), :] = both
        return carry

    lax.fori_loop(0, boxes // pair, respond, 0)
    leaving = jnp.zeros((all_rows, LANES), F32)
    for h in range(halves):
        leaving = leaving + dot(perm[h], total[h * LANES : (h + 1) * LANES, :], 1, 1)
    send3[...] = leaving.astype(BF16)

    def give_back(k, carry):
        other = lax.rem(me + k, devices)
        to_dom, to_dir = lax.div(other, dirs), lax.rem(other, dirs)
        pltpu.make_async_remote_copy(
            src_ref=send3.at[tile(to_dir * doms + to_dom)],
            dst_ref=recv3.at[tile(my_slot)],
            send_sem=send_sem.at[1],
            recv_sem=recv_sem.at[1],
            device_id=(to_dom, to_dir),
            device_id_type=MESH,
        ).start()
        return carry

    lax.fori_loop(1, devices, give_back, 0)
    recv3[tile(my_slot), :] = send3[tile(my_slot), :]

    schur(subs - 1)

    drain(recv3, recv_sem.at[1])
    group_rows = doms * unit
    field = jnp.zeros((group_rows, LANES), F32)
    for r in range(dirs):
        field = field + recv3[r * group_rows : (r + 1) * group_rows, :].astype(F32)
    back = dot(field.T.astype(BF16), place[...], 1, 0)
    sub_box = iota((LANES, amount), 0) >> shift_of(excites)
    back = jnp.where((owner_row & (per_tile - 1)) == sub_box, back, 0.0)
    back = jnp.sum(back.reshape(per_tile, excites, amount), axis=0)
    for s in range(subs):
        add = coupled[s]
        out_ref[s, :, :surface] += add[:, :surface] + back[:, s * surface : (s + 1) * surface]
        out_ref[s, :, surface:] += add[:, surface:]

    for copy in sides:
        copy.wait_send()
    for copy in wides:
        copy.wait_send()
    drain(recv1, send_sem.at[0])
    drain(recv3, send_sem.at[1])


def shards(
    mesh_dims,
    unknowns,
    schur_blocks,
    adjacency,
    row_map,
    coupling,
    owner_box,
    aggregation,
    trans_table,
    inter_list,
    inter_type,
    near_list,
    near_blocks,
):
    doms, dirs = mesh_dims
    subs, excites, rows = unknowns.shape
    boxes, slots, directions = aggregation.shape
    capacity = slots // (doms * dirs)
    per_tile = LANES // excites
    halves = boxes // per_tile
    unit = max(16, halves * capacity)
    all_rows = doms * dirs * unit
    amount = subs * owner_box.shape[1]
    vmem = pl.BlockSpec(memory_space=pltpu.VMEM)
    smem = pl.BlockSpec(memory_space=pltpu.SMEM)
    hbm = pl.BlockSpec(memory_space=pl.ANY)
    dma = pltpu.SemaphoreType.DMA
    scratch = [
        pltpu.VMEM((boxes, directions, slots), BF16),
        pltpu.VMEM(trans_table.shape, F32),
        pltpu.VMEM(trans_table.shape[::-1], F32),
        pltpu.VMEM(row_map.shape, jnp.int32),
        pltpu.VMEM(coupling.shape, F32),
        pltpu.VMEM(schur_blocks.shape, BF16),
        pltpu.VMEM(near_blocks.shape, BF16),
        pltpu.VMEM((doms * unit, amount), BF16),
        pltpu.VMEM((halves, all_rows, slots), BF16),
        pltpu.VMEM((doms * unit, LANES), BF16),
        pltpu.VMEM((all_rows, LANES), BF16),
        pltpu.VMEM((2, subs, excites, rows), BF16),
        pltpu.VMEM((3 * subs, excites, rows), F32),
        pltpu.VMEM((boxes, excites, slots), F32),
        pltpu.VMEM((boxes * excites, directions), BF16),
        pltpu.VMEM((2, boxes * excites, directions), BF16),
        pltpu.VMEM((3 * boxes, excites, directions), F32),
        pltpu.VMEM((subs, excites, rows), F32),
        pltpu.VMEM((boxes, excites, slots), F32),
        pltpu.VMEM((boxes * excites, slots), BF16),
        pltpu.VMEM((all_rows, LANES), BF16),
        pltpu.VMEM((all_rows, LANES), BF16),
        dma((5,)),
        dma((subs,)),
        dma((2,)),
        dma((2,)),
        dma((2,)),
        dma((2,)),
        dma((2, 4)),
        dma((2, 4)),
    ]
    return pl.pallas_call(
        functools.partial(kernel, mesh_dims),
        out_shape=jax.ShapeDtypeStruct(unknowns.shape, F32),
        in_specs=[smem] * 4 + [vmem] * 2 + [hbm] * 6,
        out_specs=vmem,
        scratch_shapes=scratch,
        compiler_params=pltpu.CompilerParams(
            collective_id=0, has_side_effects=True, vmem_limit_bytes=56 * 1024 * 1024
        ),
    )(
        adjacency,
        inter_list.T,
        inter_type.T,
        near_list.T,
        unknowns,
        owner_box.reshape(1, amount),
        jnp.swapaxes(aggregation, 1, 2),
        trans_table.T,
        row_map,
        coupling,
        schur_blocks,
        near_blocks,
    )


def solution(mesh):
    in_specs = (
        P(("dom", "dir"), None, None),
        P(("dom", "dir"), None, None),
        P(("dom", "dir"), None),
        P(("dom", "dir"), None, None),
        P(("dom", "dir"), None, None),
        P(("dom", "dir"), None, None),
        P("dom", None, "dir"),
        P(None, "dir"),
        P("dom", None),
        P("dom", None),
        P(("dom", "dir"), None),
        P(("dom", "dir"), None, None, None),
    )
    out_specs = P(("dom", "dir"), None, None)
    dims = (mesh.shape["dom"], mesh.shape["dir"])
    return jax.shard_map(
        functools.partial(shards, dims),
        mesh=mesh,
        in_specs=in_specs,
        out_specs=out_specs,
        check_vma=False,
    )
```

time: 159 us -> 37.3 us (0.23); the launches traced: 157 us -> 37.1 us
  matrix products: 54.7 us -> 0 us
  local copies, waits for them, and re-layouts: 45.5 us -> 1.57 us
  Pallas kernels: 0 us -> 35.5 us
  starting transfers between devices: 22 us -> 0 us
  between operations: 13.6 us -> 0.01 us
  waiting for transfers between devices: 11.8 us -> 0 us
  blocking collectives: 5.43 us -> 0 us
  other arithmetic: 3.71 us -> 0 us
    dot_general x27 -> x0, matrix products: 54.7 us -> none  [the longest x16 14.2 us: fetch_rows(): jnp.einsum('ej,ij->ei', source, selector, preferred_element_type=jnp.floa...]
    pallas_call x0 -> x1, Pallas kernels: none -> 35.5 us  [shards(): pl.pallas_call(functools.partial(kernel, mesh_dims), out_shape=jax.ShapeD...]
    unnamed x23 -> x1, local copies, waits for them, and re-layouts: 18.8 us -> 1.57 us
    dynamic_slice x16 -> x0, local copies, waits for them, and re-layouts: 12.3 us -> none  [shards(): lax.map(fetch_rows, (maps_flat, picked_flat))]
    all_to_all x3 -> x0, starting transfers between devices: 11 us -> none  [the longest x1 4.3 us: shards(): lax.all_to_all(leaving, 'dom', split_axis=3, concat_axis=0, tiled=True)]
    ppermute x4 -> x0, starting transfers between devices: 10.9 us -> none  [the longest x2 6.03 us: padded(): after = lax.ppermute(leading, axis, down)]
    all_to_all x3 -> x0, waiting for transfers between devices: 6.62 us -> none  [the longest x1 6.61 us: shards(): lax.all_to_all(leaving, 'dom', split_axis=3, concat_axis=0, tiled=True)]
    dot_general x1 -> x0, local copies, waits for them, and re-layouts: 5.9 us -> none  [shards(): weights = jnp.einsum('hjw,hjd->hwd', place_hot, factors, precision=highest)]
  transfers between devices with their start and end apart: 8 -> 0, of which waited for: 3 -> 0; matrix products, arithmetic and copies ran while one was open for 50% -> 0% of each run, Pallas kernels for 0% -> 0%
where the time goes in v1:
time: 37.3 us; the launch traced here: 37.1 us
  Pallas kernels  35.5 us (95%)
  local copies, waits for them, and re-layouts  1.57 us (4%)
    pallas_call x1, Pallas kernels, shards(): pl.pallas_call(functools.partial(kernel, mesh_dims), out_shape=jax.ShapeD...  35.5 us
    unnamed x1, local copies, waits for them, and re-layouts  1.57 us

profile of v1, /device:TPU:0, one launch (start us, length us, event | category | flops | bytes accessed | tf_op | source)
XLA Modules:
  0.0 37.1 jit_solution(12618274734712343131)
XLA Ops:
  0.0 35.5 %shard_map.118 = f32[4,8,1024]{2,1,0:T(8,128)} custom-call(s32[4,4]{1,0:T(4,128)} %adj_ref.1, s32[16,32]{1,0:T(8,128)} %bitcast.8, s32[16,32]{1,0:T(8,128)} %bitcast.9, s32[4,8]{1,0:T(4,128)} %bitcast.11, bf16[4,8,1024]{2,1,0:T(8,128)(2,1)} %unk_ref.1, s32[1,1024]{1,0:T(1,128)} %bitcast.10, bf16[32,288,256]{2,1,0:T(8,128)(2,1)} %bitcast.6, ...), custom_call_target="tpu_custom_call" | custom-call | tf_op jit(solution)/shard_map/pallas_call | solution.py:446
  35.5 1.6 %copy.14 = f32[4,8,1024]{2,1,0:T(8,128)} copy(f32[4,8,1024]{2,1,0:T(8,128)} %shard_map.118) | data formatting | bytes 262144

commit v2 on v1

--- a/solution.py
+++ b/solution.py
@@ -200,18 +200,10 @@
         copy.start()
         sides.append(copy)
 
-    block = 256
-
     def schur(s):
         schurs[s].wait()
         unknown = unk_ref[s]
-
-        def part(i, carry):
-            at = pl.ds(pl.multiple_of(i * block, block), block)
-            out_ref[s, :, at] = dot(unknown, schur_v[s, at, :], 1, 1)
-            return carry
-
-        lax.fori_loop(0, rows // block, part, 0)
+        out_ref[s] = dot(unknown, schur_v[s], 1, 1)
 
     schur(0)
     schur(1)
@@ -229,7 +221,7 @@
     locals_[0].wait()
     chunks = 4
     chunk_boxes = boxes // chunks
-    pair = 2
+    pair = 8
     wides = []
     for c in range(chunks):
 
@@ -240,8 +232,9 @@
                 b = first + k
                 found.append(dot(curf[b].astype(BF16), agg_v[b], 1, 1))
             both = jnp.concatenate(found, axis=0).astype(BF16)
-            pats[pl.ds(pl.multiple_of(first * excites, 16), 16), :] = both
-            patf[pl.ds(boxes + first, pair)] = both.astype(F32).reshape(pair, excites, directions)
+            size = pair * excites
+            pats[pl.ds(pl.multiple_of(first * excites, size), size), :] = both
+            patf[pl.ds(my_dom * boxes + first, pair)] = both.astype(F32).reshape(pair, excites, directions)
             return carry
 
         lax.fori_loop(0, chunk_boxes // pair, radiate, 0)
@@ -264,15 +257,19 @@
     locals_[4].wait()
     nearf[...] = jnp.zeros_like(nearf)
 
-    def near(b, carry):
-        field = jnp.zeros((excites, slots), F32)
-        for j in range(near_count):
-            source = curf[near_ref[j, b]].astype(BF16)
-            field = field + dot(source, blocks_v[b, j], 1, 1)
-        nearf[my_dir * own + b] = field
-        return carry
-
-    lax.fori_loop(0, own, near, 0)
+    near_pair = 4
+
+    def near(i, carry):
+        for k in range(near_pair):
+            b = i * near_pair + k
+            field = jnp.zeros((excites, slots), F32)
+            for j in range(near_count):
+                source = curf[near_ref[j, b]].astype(BF16)
+                field = field + dot(source, blocks_v[b, j], 1, 1)
+            nearf[my_dir * own + b] = field
+        return carry
+
+    lax.fori_loop(0, own // near_pair, near, 0)
 
     for copy in sides:
         copy.wait_recv()
@@ -316,10 +313,8 @@
 
     for copy in wides:
         copy.wait_recv()
-    for side, base in ((0, 0), (1, 2 * boxes)):
-        patf[base : base + boxes] = recv2[side].astype(F32).reshape(boxes, excites, directions)
-
-    box_base = left * boxes
+    for side, source in enumerate((left, right)):
+        patf[pl.ds(source * boxes, boxes)] = recv2[side].astype(F32).reshape(boxes, excites, directions)
 
     def respond(i, carry):
         first = i * pair
@@ -328,13 +323,11 @@
             b = first + k
             field = jnp.zeros((excites, directions), F32)
             for j in range(list_len):
-                offset = list_ref[j, b] - box_base
-                offset = jnp.where(offset < 0, offset + boxes * doms, offset)
-                offset = jnp.minimum(offset, 3 * boxes - 1)
-                field = field + trans_v[pl.ds(type_ref[j, b], 1), :] * patf[offset]
+                field = field + trans_v[pl.ds(type_ref[j, b], 1), :] * patf[list_ref[j, b]]
             found.append(dot(field.astype(BF16), agg_v[b], 1, 0) + nearf[b])
         both = jnp.concatenate(found, axis=0).astype(BF16)
-        total[pl.ds(pl.multiple_of(first * excites, 16), 16), :] = both
+        size = pair * excites
+        total[pl.ds(pl.multiple_of(first * excites, size), size), :] = both
         return carry
 
     lax.fori_loop(0, boxes // pair, respond, 0)
@@ -428,7 +421,7 @@
         pltpu.VMEM((boxes, excites, slots), F32),
         pltpu.VMEM((boxes * excites, directions), BF16),
         pltpu.VMEM((2, boxes * excites, directions), BF16),
-        pltpu.VMEM((3 * boxes, excites, directions), F32),
+        pltpu.VMEM((doms * boxes, excites, directions), F32),
         pltpu.VMEM((subs, excites, rows), F32),
         pltpu.VMEM((boxes, excites, slots), F32),
         pltpu.VMEM((boxes * excites, slots), BF16),
@@ -450,7 +443,7 @@
         out_specs=vmem,
         scratch_shapes=scratch,
         compiler_params=pltpu.CompilerParams(
-            collective_id=0, has_side_effects=True, vmem_limit_bytes=56 * 1024 * 1024
+            collective_id=0, has_side_effects=True, vmem_limit_bytes=52 * 1024 * 1024
         ),
     )(
         adjacency,

time: 37.3 us -> 40.1 us (1.075)
  local copies, waits for them, and re-layouts: 1.57 us -> 7.63 us
  Pallas kernels: 35.5 us -> 32 us
    unnamed x1 -> x19, local copies, waits for them, and re-layouts: 1.57 us -> 7.63 us
    pallas_call x1, Pallas kernels: 35.5 us -> 32 us  [shards(): pl.pallas_call(functools.partial(kernel, mesh_dims), out_shape=jax.ShapeD...]
where the time goes in v2:
time: 40.1 us; the launch traced here: 39.6 us
  Pallas kernels  32 us (80%)
  local copies, waits for them, and re-layouts  7.63 us (19%)
    pallas_call x1, Pallas kernels, shards(): pl.pallas_call(functools.partial(kernel, mesh_dims), out_shape=jax.ShapeD...  32 us
    unnamed x19, local copies, waits for them, and re-layouts  7.63 us

profile of v2, /device:TPU:0, one launch (start us, length us, event | category | flops | bytes accessed | tf_op | source)
XLA Modules:
  0.0 39.6 jit_solution(6239073119873724242)
XLA Ops:
  0.0 0.0 copy-start
  0.0 1.0 %copy-done = f32[316,288]{0,1:T(8,128)S(1)} copy-done((f32[316,288]{0,1:T(8,128)S(1)}, f32[316,288]{0,1:T(8,128)}, u32[]{:S(2)}) %copy-start) | copy-done | bytes 364056
  1.0 0.0 copy-start.1
  1.0 0.8 %copy-done.1 = bf16[4,8,1024]{2,1,0:T(8,128)(2,1)S(1)} copy-done((bf16[4,8,1024]{2,1,0:T(8,128)(2,1)S(1)}, bf16[4,8,1024]{2,1,0:T(8,128)(2,1)}, u32[]{:S(2)}) %copy-start.1) | copy-done | bytes 65560
  1.9 0.0 copy-start.2
  1.9 0.8 %copy-done.2 = s32[4,4,1024]{2,1,0:T(4,128)S(1)} copy-done((s32[4,4,1024]{2,1,0:T(4,128)S(1)}, s32[4,4,1024]{2,1,0:T(4,128)}, u32[]{:S(2)}) %copy-start.2) | copy-done | bytes 65560
  2.7 0.0 copy-start.3
  2.7 0.8 %copy-done.3 = f32[4,4,1024]{2,1,0:T(4,128)S(1)} copy-done((f32[4,4,1024]{2,1,0:T(4,128)S(1)}, f32[4,4,1024]{2,1,0:T(4,128)}, u32[]{:S(2)}) %copy-start.3) | copy-done | bytes 65560
  3.5 0.0 copy-start.4
  3.5 0.7 %copy-done.4 = s32[32,16]{0,1:T(8,128)S(1)} copy-done((s32[32,16]{0,1:T(8,128)S(1)}, s32[32,16]{0,1:T(8,128)}, u32[]{:S(2)}) %copy-start.4) | copy-done | bytes 2072
  4.2 0.0 copy-start.5
  4.2 0.7 %copy-done.5 = s32[32,16]{0,1:T(8,128)S(1)} copy-done((s32[32,16]{0,1:T(8,128)S(1)}, s32[32,16]{0,1:T(8,128)}, u32[]{:S(2)}) %copy-start.5) | copy-done | bytes 2072
  4.9 0.0 copy-start.6
  4.9 0.7 %copy-done.6 = s32[4,256,1]{1,2,0:T(1,128)S(1)} copy-done((s32[4,256,1]{1,2,0:T(1,128)S(1)}, s32[4,256,1]{1,2,0:T(1,128)}, u32[]{:S(2)}) %copy-start.6) | copy-done | bytes 4120
  5.6 0.0 copy-start.7
  5.6 0.7 %copy-done.7 = s32[4,4]{1,0:T(4,128)S(1)} copy-done((s32[4,4]{1,0:T(4,128)S(1)}, s32[4,4]{1,0:T(4,128)}, u32[]{:S(2)}) %copy-start.7) | copy-done | bytes 88
  6.3 0.0 copy-start.8
  6.3 0.7 %copy-done.8 = s32[8,4]{0,1:T(4,128)S(1)} copy-done((s32[8,4]{0,1:T(4,128)S(1)}, s32[8,4]{0,1:T(4,128)}, u32[]{:S(2)}) %copy-start.8) | copy-done | bytes 152
  7.0 32.0 %shard_map.118 = f32[4,8,1024]{2,1,0:T(8,128)S(1)} custom-call(s32[4,4]{1,0:T(4,128)S(1)} %copy-done.7, s32[16,32]{1,0:T(8,128)S(1)} %bitcast.7, s32[16,32]{1,0:T(8,128)S(1)} %bitcast.8, s32[4,8]{1,0:T(4,128)S(1)} %bitcast.10, bf16[4,8,1024]{2,1,0:T(8,128)(2,1)S(1)} %copy-done.1, s32[1,1024]{1,0:T(1,128)S(1)} %bitcast.9, bf16[32,288,256]{2,1,0:T(8,128)(2,1)} %bitcast.11, ...), custom_call_target="tpu_custom_call" | custom-call | tf_op jit(solution)/shard_map/pallas_call | solution.py:439
  38.9 0.7 %copy.14 = f32[4,8,1024]{2,1,0:T(8,128)} copy(f32[4,8,1024]{2,1,0:T(8,128)S(1)} %shard_map.118) | data formatting | bytes 262144
Async XLA Ops:
  0.0 1.0 %copy-start = (f32[316,288]{0,1:T(8,128)S(1)}, f32[316,288]{0,1:T(8,128)}, u32[]{:S(2)}) copy-start(f32[316,288]{0,1:T(8,128)} %param.19) | copy-start | bytes 1092100
  1.0 0.8 %copy-start.1 = (bf16[4,8,1024]{2,1,0:T(8,128)(2,1)S(1)}, bf16[4,8,1024]{2,1,0:T(8,128)(2,1)}, u32[]{:S(2)}) copy-start(bf16[4,8,1024]{2,1,0:T(8,128)(2,1)} %unk_ref.1) | copy-start | bytes 196612
  1.9 0.8 %copy-start.2 = (s32[4,4,1024]{2,1,0:T(4,128)S(1)}, s32[4,4,1024]{2,1,0:T(4,128)}, u32[]{:S(2)}) copy-start(s32[4,4,1024]{2,1,0:T(4,128)} %maps_hbm.1) | copy-start | bytes 196612
  2.7 0.8 %copy-start.3 = (f32[4,4,1024]{2,1,0:T(4,128)S(1)}, f32[4,4,1024]{2,1,0:T(4,128)}, u32[]{:S(2)}) copy-start(f32[4,4,1024]{2,1,0:T(4,128)} %coup_hbm.1) | copy-start | bytes 196612
  3.5 0.7 %copy-start.4 = (s32[32,16]{0,1:T(8,128)S(1)}, s32[32,16]{0,1:T(8,128)}, u32[]{:S(2)}) copy-start(s32[32,16]{0,1:T(8,128)} %param.20) | copy-start | bytes 6148
  4.2 0.7 %copy-start.5 = (s32[32,16]{0,1:T(8,128)S(1)}, s32[32,16]{0,1:T(8,128)}, u32[]{:S(2)}) copy-start(s32[32,16]{0,1:T(8,128)} %param.21) | copy-start | bytes 6148
  4.9 0.7 %copy-start.6 = (s32[4,256,1]{1,2,0:T(1,128)S(1)}, s32[4,256,1]{1,2,0:T(1,128)}, u32[]{:S(2)}) copy-start(s32[4,256,1]{1,2,0:T(1,128)} %param.17) | copy-start | bytes 12292
  5.6 0.7 %copy-start.7 = (s32[4,4]{1,0:T(4,128)S(1)}, s32[4,4]{1,0:T(4,128)}, u32[]{:S(2)}) copy-start(s32[4,4]{1,0:T(4,128)} %adj_ref.1) | copy-start | bytes 196
  6.3 0.7 %copy-start.8 = (s32[8,4]{0,1:T(4,128)S(1)}, s32[8,4]{0,1:T(4,128)}, u32[]{:S(2)}) copy-start(s32[8,4]{0,1:T(4,128)} %param.22) | copy-start | bytes 388

commit v3 on v2

--- a/solution.py
+++ b/solution.py
@@ -29,10 +29,10 @@
 
 def kernel(
     dims,
-    adj_ref,
-    list_ref,
-    type_ref,
-    near_ref,
+    adj_hbm,
+    list_hbm,
+    type_hbm,
+    near_hbm,
     unk_ref,
     owner_ref,
     agg_hbm,
@@ -42,6 +42,10 @@
     schur_hbm,
     blocks_hbm,
     out_ref,
+    adj_ref,
+    list_ref,
+    type_ref,
+    near_ref,
     agg_v,
     trans_v,
     trans_t,
@@ -92,6 +96,11 @@
     me = my_dom * dirs + my_dir
     my_slot = my_dir * doms + my_dom
     right, left = lax.rem(my_dom + 1, doms), lax.rem(my_dom + doms - 1, doms)
+    odd = lax.rem(my_dom, 2)
+    partner = my_dom + 1 - 2 * odd
+    relay_to = lax.rem(my_dom + 2 - 4 * odd + doms, doms)
+    relay_from = lax.rem(my_dom - 2 + 4 * odd + doms, doms)
+    relay_source = relay_from + 1 - 2 * odd
 
     barrier = pltpu.get_barrier_semaphore()
 
@@ -116,6 +125,10 @@
                 (maps_hbm, maps_v),
                 (coup_hbm, coup_v),
                 (blocks_hbm, blocks_v),
+                (adj_hbm, adj_ref),
+                (list_hbm, list_ref),
+                (type_hbm, type_ref),
+                (near_hbm, near_ref),
             ]
         )
     ]
@@ -126,7 +139,7 @@
     schurs[0].start()
     schurs[1].start()
     locals_[4].start()
-    for i in (1, 2, 3):
+    for i in (1, 2, 3, 5, 6, 7, 8):
         locals_[i].start()
     for s in range(2, subs):
         schurs[s].start()
@@ -239,45 +252,61 @@
 
         lax.fori_loop(0, chunk_boxes // pair, radiate, 0)
         at = pl.ds(c * chunk_boxes * excites, chunk_boxes * excites)
-        for side, target in enumerate((right, left)):
-            copy = pltpu.make_async_remote_copy(
-                src_ref=pats.at[at],
-                dst_ref=recv2.at[side, at],
-                send_sem=wide_send.at[side, c],
-                recv_sem=wide_recv.at[side, c],
-                device_id=(target, my_dir),
-                device_id_type=MESH,
-            )
-            copy.start()
-            wides.append(copy)
-
-    locals_[1].wait()
+        copy = pltpu.make_async_remote_copy(
+            src_ref=pats.at[at],
+            dst_ref=recv2.at[0, at],
+            send_sem=wide_send.at[0, c],
+            recv_sem=wide_recv.at[0, c],
+            device_id=(partner, my_dir),
+            device_id_type=MESH,
+        )
+        copy.start()
+        wides.append(copy)
+
+    relays = []
+
+    def relay(c):
+        wides[c].wait_recv()
+        at = pl.ds(c * chunk_boxes * excites, chunk_boxes * excites)
+        copy = pltpu.make_async_remote_copy(
+            src_ref=recv2.at[0, at],
+            dst_ref=recv2.at[1, at],
+            send_sem=wide_send.at[1, c],
+            recv_sem=wide_recv.at[1, c],
+            device_id=(relay_to, my_dir),
+            device_id_type=MESH,
+        )
+        copy.start()
+        relays.append(copy)
+
+    for i in (1, 2, 3, 5, 6, 7, 8):
+        locals_[i].wait()
     trans_v[...] = trans_t[...].T
 
     locals_[4].wait()
     nearf[...] = jnp.zeros_like(nearf)
 
-    near_pair = 4
-
-    def near(i, carry):
-        for k in range(near_pair):
-            b = i * near_pair + k
-            field = jnp.zeros((excites, slots), F32)
-            for j in range(near_count):
-                source = curf[near_ref[j, b]].astype(BF16)
-                field = field + dot(source, blocks_v[b, j], 1, 1)
-            nearf[my_dir * own + b] = field
-        return carry
-
-    lax.fori_loop(0, own // near_pair, near, 0)
+    def near(b):
+        field = jnp.zeros((excites, slots), F32)
+        for j in range(near_count):
+            source = curf[near_ref[j, b]].astype(BF16)
+            field = field + dot(source, blocks_v[b, j], 1, 1)
+        nearf[my_dir * own + b] = field
+
+    relay(0)
+    for b in range(own // 2):
+        near(b)
+    relay(1)
+    for b in range(own // 2, own):
+        near(b)
+    relay(2)
 
     for copy in sides:
         copy.wait_recv()
     winf[0:subs] = recv0[0].astype(F32)
     winf[subs : 2 * subs] = unk_ref[...].astype(F32)
     winf[2 * subs : 3 * subs] = recv0[1].astype(F32)
-    locals_[2].wait()
-    locals_[3].wait()
+    relay(3)
     group_subs = subs * dirs
     sub_base = left * group_subs
 
@@ -311,9 +340,9 @@
     for s in range(2, subs - 1):
         schur(s)
 
-    for copy in wides:
+    for copy in relays:
         copy.wait_recv()
-    for side, source in enumerate((left, right)):
+    for side, source in enumerate((partner, relay_source)):
         patf[pl.ds(source * boxes, boxes)] = recv2[side].astype(F32).reshape(boxes, excites, directions)
 
     def respond(i, carry):
@@ -370,7 +399,7 @@
 
     for copy in sides:
         copy.wait_send()
-    for copy in wides:
+    for copy in wides + relays:
         copy.wait_send()
     drain(recv1, send_sem.at[0])
     drain(recv3, send_sem.at[1])
@@ -401,10 +430,13 @@
     all_rows = doms * dirs * unit
     amount = subs * owner_box.shape[1]
     vmem = pl.BlockSpec(memory_space=pltpu.VMEM)
-    smem = pl.BlockSpec(memory_space=pltpu.SMEM)
     hbm = pl.BlockSpec(memory_space=pl.ANY)
     dma = pltpu.SemaphoreType.DMA
-    scratch = [
+    smem = [
+        pltpu.SMEM(value.shape, jnp.int32)
+        for value in (adjacency, inter_list.T, inter_type.T, near_list.T)
+    ]
+    scratch = smem + [
         pltpu.VMEM((boxes, directions, slots), BF16),
         pltpu.VMEM(trans_table.shape, F32),
         pltpu.VMEM(trans_table.shape[::-1], F32),
@@ -427,7 +459,7 @@
         pltpu.VMEM((boxes * excites, slots), BF16),
         pltpu.VMEM((all_rows, LANES), BF16),
         pltpu.VMEM((all_rows, LANES), BF16),
-        dma((5,)),
+        dma((9,)),
         dma((subs,)),
         dma((2,)),
         dma((2,)),
@@ -438,12 +470,12 @@
     ]
     return pl.pallas_call(
         functools.partial(kernel, mesh_dims),
-        out_shape=jax.ShapeDtypeStruct(unknowns.shape, F32),
-        in_specs=[smem] * 4 + [vmem] * 2 + [hbm] * 6,
+        out_shape=pltpu.VMEM(unknowns.shape, F32),
+        in_specs=[hbm] * 4 + [vmem] * 2 + [hbm] * 6,
         out_specs=vmem,
         scratch_shapes=scratch,
         compiler_params=pltpu.CompilerParams(
-            collective_id=0, has_side_effects=True, vmem_limit_bytes=52 * 1024 * 1024
+            collective_id=0, has_side_effects=True, vmem_limit_bytes=56 * 1024 * 1024
         ),
     )(
         adjacency,

time: 40.1 us -> 32.1 us (0.80)
  local copies, waits for them, and re-layouts: 7.63 us -> 0.66 us
  Pallas kernels: 32 us -> 31.3 us
    unnamed x19 -> x1, local copies, waits for them, and re-layouts: 7.63 us -> 0.66 us
    pallas_call x1, Pallas kernels: 32 us -> 31.3 us  [shards(): pl.pallas_call(functools.partial(kernel, mesh_dims), out_shape=pltpu.VMEM...]
where the time goes in v3:
time: 32.1 us; the launch traced here: 32 us
  Pallas kernels  31.3 us (98%)
  local copies, waits for them, and re-layouts  0.66 us (2%)
    pallas_call x1, Pallas kernels, shards(): pl.pallas_call(functools.partial(kernel, mesh_dims), out_shape=pltpu.VMEM...  31.3 us
    unnamed x1, local copies, waits for them, and re-layouts  0.66 us

profile of v3, /device:TPU:0, one launch (start us, length us, event | category | flops | bytes accessed | tf_op | source)
XLA Modules:
  0.0 32.0 jit_solution(6541474380088046528)
XLA Ops:
  0.0 31.3 %shard_map.118 = f32[4,8,1024]{2,1,0:T(8,128)S(1)} custom-call(s32[4,4]{1,0:T(4,128)} %adj_hbm.1, s32[16,32]{1,0:T(8,128)} %bitcast.8, s32[16,32]{1,0:T(8,128)} %bitcast.9, s32[4,8]{1,0:T(4,128)} %bitcast.11, bf16[4,8,1024]{2,1,0:T(8,128)(2,1)} %unk_ref.1, s32[1,1024]{1,0:T(1,128)} %bitcast.10, bf16[32,288,256]{2,1,0:T(8,128)(2,1)} %bitcast.6, ...), custom_call_target="tpu_custom_call" | custom-call | tf_op jit(solution)/shard_map/pallas_call | solution.py:471
  31.3 0.7 %copy.14 = f32[4,8,1024]{2,1,0:T(8,128)} copy(f32[4,8,1024]{2,1,0:T(8,128)S(1)} %shard_map.118) | data formatting | bytes 262144

commit v4 on v3

--- a/solution.py
+++ b/solution.py
@@ -138,11 +138,7 @@
     locals_[0].start()
     schurs[0].start()
     schurs[1].start()
-    locals_[4].start()
-    for i in (1, 2, 3, 5, 6, 7, 8):
-        locals_[i].start()
-    for s in range(2, subs):
-        schurs[s].start()
+    locals_[1].start()
 
     owner_row = owner_ref[...]
     owner_col = jnp.concatenate(
@@ -152,12 +148,16 @@
         ],
         axis=0,
     )
-    order = iota((amount, LANES), 0)
-    ahead = order - iota((amount, LANES), 1)
+    ahead = iota((LANES, LANES), 0) < iota((LANES, LANES), 1)
     ranks = []
     for k in range(0, amount, LANES):
-        same = (owner_col == owner_row[:, k : k + LANES]) & (ahead < k)
-        ranks.append(jnp.sum(jnp.where(same, 1.0, 0.0), axis=0, keepdims=True))
+        piece = owner_row[:, k : k + LANES]
+        same = (owner_col[k : k + LANES] == piece) & ahead
+        count = jnp.sum(jnp.where(same, 1.0, 0.0), axis=0, keepdims=True)
+        if k > 0:
+            earlier = jnp.where(owner_col[:k] == piece, 1.0, 0.0)
+            count = count + jnp.sum(earlier, axis=0, keepdims=True)
+        ranks.append(count)
     rank = jnp.concatenate(ranks, axis=1).astype(jnp.int32)
     half = (owner_row & (boxes - 1)) >> shift_of(per_tile)
     key = (owner_row >> shift_of(boxes)) * unit + half * capacity + rank
@@ -171,14 +171,6 @@
     wide = jnp.where((owner_col & (per_tile - 1)) == lane_box, wide, 0.0).astype(BF16)
     send1[...] = dot(place[...], wide, 1, 0).astype(BF16)
 
-    row = iota((all_rows, slots), 0)
-    col = iota((all_rows, slots), 1)
-    within = row & (unit - 1)
-    slot_of = (row >> shift_of(unit)) * capacity + (within & (capacity - 1))
-    for h in range(halves):
-        hit = (slot_of == col) & ((within >> shift_of(capacity)) == h)
-        perm[h] = jnp.where(hit, 1.0, 0.0).astype(BF16)
-
     pl.semaphore_wait(barrier, devices - 1)
 
     def tile(index):
@@ -200,6 +192,75 @@
     lax.fori_loop(1, devices, scatter, 0)
     recv1[tile(my_slot), :] = send1[tile(my_dom), :]
 
+    locals_[4].start()
+    for s in range(2, subs):
+        schurs[s].start()
+    for i in (2, 3, 5, 6, 7, 8):
+        locals_[i].start()
+
+    row = iota((all_rows, slots), 0)
+    col = iota((all_rows, slots), 1)
+    within = row & (unit - 1)
+    slot_of = (row >> shift_of(unit)) * capacity + (within & (capacity - 1))
+    for h in range(halves):
+        hit = (slot_of == col) & ((within >> shift_of(capacity)) == h)
+        perm[h] = jnp.where(hit, 1.0, 0.0).astype(BF16)
+
+    def schur(s):
+        schurs[s].wait()
+        unknown = unk_ref[s]
+        out_ref[s] = dot(unknown, schur_v[s], 1, 1)
+
+    schur(0)
+    schur(1)
+    locals_[1].wait()
+    turned = trans_t[...].T
+    trans_v[...] = jnp.broadcast_to(
+        turned[:, None, :], (turned.shape[0], excites, turned.shape[1])
+    )
+
+    def drain(buffer, sem):
+        size = pl.ds(0, all_rows - unit)
+        pltpu.make_async_copy(buffer.at[size], buffer.at[size], sem).wait()
+
+    drain(recv1, recv_sem.at[0])
+    arrived = recv1[...]
+    for h in range(halves):
+        piece = dot(arrived, perm[h], 0, 0)
+        curf[h * per_tile : (h + 1) * per_tile] = piece.reshape(per_tile, excites, slots)
+
+    locals_[0].wait()
+    chunks = 4
+    chunk_boxes = boxes // chunks
+    pair = 8
+    wides = []
+    for c in range(chunks):
+
+        def radiate(i, carry):
+            first = c * chunk_boxes + i * pair
+            found = []
+            for k in range(pair):
+                b = first + k
+                found.append(dot(curf[b].astype(BF16), agg_v[b], 1, 1))
+            both = jnp.concatenate(found, axis=0).astype(BF16)
+            size = pair * excites
+            pats[pl.ds(pl.multiple_of(first * excites, size), size), :] = both
+            patf[pl.ds(my_dom * boxes + first, pair)] = both.astype(F32).reshape(pair, excites, directions)
+            return carry
+
+        lax.fori_loop(0, chunk_boxes // pair, radiate, 0)
+        at = pl.ds(c * chunk_boxes * excites, chunk_boxes * excites)
+        copy = pltpu.make_async_remote_copy(
+            src_ref=pats.at[at],
+            dst_ref=recv2.at[0, at],
+            send_sem=wide_send.at[0, c],
+            recv_sem=wide_recv.at[0, c],
+            device_id=(partner, my_dir),
+            device_id_type=MESH,
+        )
+        copy.start()
+        wides.append(copy)
+
     sides = []
     for side, target in enumerate((right, left)):
         copy = pltpu.make_async_remote_copy(
@@ -212,56 +273,6 @@
         )
         copy.start()
         sides.append(copy)
-
-    def schur(s):
-        schurs[s].wait()
-        unknown = unk_ref[s]
-        out_ref[s] = dot(unknown, schur_v[s], 1, 1)
-
-    schur(0)
-    schur(1)
-
-    def drain(buffer, sem):
-        size = pl.ds(0, all_rows - unit)
-        pltpu.make_async_copy(buffer.at[size], buffer.at[size], sem).wait()
-
-    drain(recv1, recv_sem.at[0])
-    arrived = recv1[...]
-    for h in range(halves):
-        piece = dot(arrived, perm[h], 0, 0)
-        curf[h * per_tile : (h + 1) * per_tile] = piece.reshape(per_tile, excites, slots)
-
-    locals_[0].wait()
-    chunks = 4
-    chunk_boxes = boxes // chunks
-    pair = 8
-    wides = []
-    for c in range(chunks):
-
-        def radiate(i, carry):
-            first = c * chunk_boxes + i * pair
-            found = []
-            for k in range(pair):
-                b = first + k
-                found.append(dot(curf[b].astype(BF16), agg_v[b], 1, 1))
-            both = jnp.concatenate(found, axis=0).astype(BF16)
-            size = pair * excites
-            pats[pl.ds(pl.multiple_of(first * excites, size), size), :] = both
-            patf[pl.ds(my_dom * boxes + first, pair)] = both.astype(F32).reshape(pair, excites, directions)
-            return carry
-
-        lax.fori_loop(0, chunk_boxes // pair, radiate, 0)
-        at = pl.ds(c * chunk_boxes * excites, chunk_boxes * excites)
-        copy = pltpu.make_async_remote_copy(
-            src_ref=pats.at[at],
-            dst_ref=recv2.at[0, at],
-            send_sem=wide_send.at[0, c],
-            recv_sem=wide_recv.at[0, c],
-            device_id=(partner, my_dir),
-            device_id_type=MESH,
-        )
-        copy.start()
-        wides.append(copy)
 
     relays = []
 
@@ -279,9 +290,8 @@
         copy.start()
         relays.append(copy)
 
-    for i in (1, 2, 3, 5, 6, 7, 8):
+    for i in (2, 3, 5, 6, 7, 8):
         locals_[i].wait()
-    trans_v[...] = trans_t[...].T
 
     locals_[4].wait()
     nearf[...] = jnp.zeros_like(nearf)
@@ -294,19 +304,61 @@
         nearf[my_dir * own + b] = field
 
     relay(0)
-    for b in range(own // 2):
+    for b in range(own):
         near(b)
-    relay(1)
-    for b in range(own // 2, own):
-        near(b)
-    relay(2)
+        if b + 1 in (own // 2, own * 3 // 4, own):
+            relay((own // 2, own * 3 // 4, own).index(b + 1) + 1)
+    for s in range(2, subs - 1):
+        schur(s)
+
+    for copy in relays:
+        copy.wait_recv()
+    for side, source in enumerate((partner, relay_source)):
+        patf[pl.ds(source * boxes, boxes)] = recv2[side].astype(F32).reshape(boxes, excites, directions)
+
+    def respond(i, carry):
+        first = i * pair
+        found = []
+        for k in range(pair):
+            b = first + k
+            field = jnp.zeros((excites, directions), F32)
+            for j in range(list_len):
+                field = field + trans_v[type_ref[j, b]] * patf[list_ref[j, b]]
+            found.append(dot(field.astype(BF16), agg_v[b], 1, 0) + nearf[b])
+        both = jnp.concatenate(found, axis=0).astype(BF16)
+        size = pair * excites
+        total[pl.ds(pl.multiple_of(first * excites, size), size), :] = both
+        return carry
+
+    lax.fori_loop(0, boxes // pair, respond, 0)
+    leaving = jnp.zeros((all_rows, LANES), F32)
+    for h in range(halves):
+        leaving = leaving + dot(perm[h], total[h * LANES : (h + 1) * LANES, :], 1, 1)
+    send3[...] = leaving.astype(BF16)
+
+    def give_back(k, carry):
+        other = lax.rem(me + k, devices)
+        to_dom, to_dir = lax.div(other, dirs), lax.rem(other, dirs)
+        pltpu.make_async_remote_copy(
+            src_ref=send3.at[tile(to_dir * doms + to_dom)],
+            dst_ref=recv3.at[tile(my_slot)],
+            send_sem=send_sem.at[1],
+            recv_sem=recv_sem.at[1],
+            device_id=(to_dom, to_dir),
+            device_id_type=MESH,
+        ).start()
+        return carry
+
+    lax.fori_loop(1, devices, give_back, 0)
+    recv3[tile(my_slot), :] = send3[tile(my_slot), :]
+
+    schur(subs - 1)
 
     for copy in sides:
         copy.wait_recv()
     winf[0:subs] = recv0[0].astype(F32)
     winf[subs : 2 * subs] = unk_ref[...].astype(F32)
     winf[2 * subs : 3 * subs] = recv0[1].astype(F32)
-    relay(3)
     group_subs = subs * dirs
     sub_base = left * group_subs
 
@@ -337,51 +389,6 @@
         return carry
 
     lax.fori_loop(0, subs, couple, 0)
-    for s in range(2, subs - 1):
-        schur(s)
-
-    for copy in relays:
-        copy.wait_recv()
-    for side, source in enumerate((partner, relay_source)):
-        patf[pl.ds(source * boxes, boxes)] = recv2[side].astype(F32).reshape(boxes, excites, directions)
-
-    def respond(i, carry):
-        first = i * pair
-        found = []
-        for k in range(pair):
-            b = first + k
-            field = jnp.zeros((excites, directions), F32)
-            for j in range(list_len):
-                field = field + trans_v[pl.ds(type_ref[j, b], 1), :] * patf[list_ref[j, b]]
-            found.append(dot(field.astype(BF16), agg_v[b], 1, 0) + nearf[b])
-        both = jnp.concatenate(found, axis=0).astype(BF16)
-        size = pair * excites
-        total[pl.ds(pl.multiple_of(first * excites, size), size), :] = both
-        return carry
-
-    lax.fori_loop(0, boxes // pair, respond, 0)
-    leaving = jnp.zeros((all_rows, LANES), F32)
-    for h in range(halves):
-        leaving = leaving + dot(perm[h], total[h * LANES : (h + 1) * LANES, :], 1, 1)
-    send3[...] = leaving.astype(BF16)
-
-    def give_back(k, carry):
-        other = lax.rem(me + k, devices)
-        to_dom, to_dir = lax.div(other, dirs), lax.rem(other, dirs)
-        pltpu.make_async_remote_copy(
-            src_ref=send3.at[tile(to_dir * doms + to_dom)],
-            dst_ref=recv3.at[tile(my_slot)],
-            send_sem=send_sem.at[1],
-            recv_sem=recv_sem.at[1],
-            device_id=(to_dom, to_dir),
-            device_id_type=MESH,
-        ).start()
-        return carry
-
-    lax.fori_loop(1, devices, give_back, 0)
-    recv3[tile(my_slot), :] = send3[tile(my_slot), :]
-
-    schur(subs - 1)
 
     drain(recv3, recv_sem.at[1])
     group_rows = doms * unit
@@ -438,7 +445,7 @@
     ]
     scratch = smem + [
         pltpu.VMEM((boxes, directions, slots), BF16),
-        pltpu.VMEM(trans_table.shape, F32),
+        pltpu.VMEM((trans_table.shape[0], excites, trans_table.shape[1]), F32),
         pltpu.VMEM(trans_table.shape[::-1], F32),
         pltpu.VMEM(row_map.shape, jnp.int32),
         pltpu.VMEM(coupling.shape, F32),

time: 32.1 us -> 33.2 us (1.034)
  Pallas kernels: 31.3 us -> 32.4 us
    pallas_call x1, Pallas kernels: 31.3 us -> 32.4 us  [shards(): pl.pallas_call(functools.partial(kernel, mesh_dims), out_shape=pltpu.VMEM...]
where the time goes in v4:
time: 33.2 us; the launch traced here: 33.1 us
  Pallas kernels  32.4 us (98%)
  local copies, waits for them, and re-layouts  0.66 us (2%)
    pallas_call x1, Pallas kernels, shards(): pl.pallas_call(functools.partial(kernel, mesh_dims), out_shape=pltpu.VMEM...  32.4 us

profile of v4, /device:TPU:0, one launch (start us, length us, event | category | flops | bytes accessed | tf_op | source)
XLA Modules:
  0.0 33.1 jit_solution(16989464472493992339)
XLA Ops:
  0.0 32.4 %shard_map.118 = f32[4,8,1024]{2,1,0:T(8,128)S(1)} custom-call(s32[4,4]{1,0:T(4,128)} %adj_hbm.1, s32[16,32]{1,0:T(8,128)} %bitcast.8, s32[16,32]{1,0:T(8,128)} %bitcast.9, s32[4,8]{1,0:T(4,128)} %bitcast.11, bf16[4,8,1024]{2,1,0:T(8,128)(2,1)} %unk_ref.1, s32[1,1024]{1,0:T(1,128)} %bitcast.10, bf16[32,288,256]{2,1,0:T(8,128)(2,1)} %bitcast.6, ...), custom_call_target="tpu_custom_call" | custom-call | tf_op jit(solution)/shard_map/pallas_call | solution.py:478
  32.4 0.7 %copy.14 = f32[4,8,1024]{2,1,0:T(8,128)} copy(f32[4,8,1024]{2,1,0:T(8,128)S(1)} %shard_map.118) | data formatting | bytes 262144

commit v5 on v3

--- a/solution.py
+++ b/solution.py
@@ -152,12 +152,16 @@
         ],
         axis=0,
     )
-    order = iota((amount, LANES), 0)
-    ahead = order - iota((amount, LANES), 1)
+    ahead = iota((LANES, LANES), 0) < iota((LANES, LANES), 1)
     ranks = []
     for k in range(0, amount, LANES):
-        same = (owner_col == owner_row[:, k : k + LANES]) & (ahead < k)
-        ranks.append(jnp.sum(jnp.where(same, 1.0, 0.0), axis=0, keepdims=True))
+        piece = owner_row[:, k : k + LANES]
+        same = (owner_col[k : k + LANES] == piece) & ahead
+        count = jnp.sum(jnp.where(same, 1.0, 0.0), axis=0, keepdims=True)
+        if k > 0:
+            earlier = jnp.where(owner_col[:k] == piece, 1.0, 0.0)
+            count = count + jnp.sum(earlier, axis=0, keepdims=True)
+        ranks.append(count)
     rank = jnp.concatenate(ranks, axis=1).astype(jnp.int32)
     half = (owner_row & (boxes - 1)) >> shift_of(per_tile)
     key = (owner_row >> shift_of(boxes)) * unit + half * capacity + rank
@@ -171,14 +175,6 @@
     wide = jnp.where((owner_col & (per_tile - 1)) == lane_box, wide, 0.0).astype(BF16)
     send1[...] = dot(place[...], wide, 1, 0).astype(BF16)
 
-    row = iota((all_rows, slots), 0)
-    col = iota((all_rows, slots), 1)
-    within = row & (unit - 1)
-    slot_of = (row >> shift_of(unit)) * capacity + (within & (capacity - 1))
-    for h in range(halves):
-        hit = (slot_of == col) & ((within >> shift_of(capacity)) == h)
-        perm[h] = jnp.where(hit, 1.0, 0.0).astype(BF16)
-
     pl.semaphore_wait(barrier, devices - 1)
 
     def tile(index):
@@ -212,6 +208,14 @@
         )
         copy.start()
         sides.append(copy)
+
+    row = iota((all_rows, slots), 0)
+    col = iota((all_rows, slots), 1)
+    within = row & (unit - 1)
+    slot_of = (row >> shift_of(unit)) * capacity + (within & (capacity - 1))
+    for h in range(halves):
+        hit = (slot_of == col) & ((within >> shift_of(capacity)) == h)
+        perm[h] = jnp.where(hit, 1.0, 0.0).astype(BF16)
 
     def schur(s):
         schurs[s].wait()
@@ -279,9 +283,8 @@
         copy.start()
         relays.append(copy)
 
-    for i in (1, 2, 3, 5, 6, 7, 8):
+    for i in (2, 3, 5, 6, 7, 8):
         locals_[i].wait()
-    trans_v[...] = trans_t[...].T
 
     locals_[4].wait()
     nearf[...] = jnp.zeros_like(nearf)
@@ -294,19 +297,20 @@
         nearf[my_dir * own + b] = field
 
     relay(0)
-    for b in range(own // 2):
+    locals_[1].wait()
+    turned = trans_t[...].T
+    trans_v[...] = jnp.broadcast_to(
+        turned[:, None, :], (turned.shape[0], excites, turned.shape[1])
+    )
+    for b in range(own):
         near(b)
-    relay(1)
-    for b in range(own // 2, own):
-        near(b)
-    relay(2)
-
+        if b + 1 in (own // 2, own * 3 // 4, own):
+            relay((own // 2, own * 3 // 4, own).index(b + 1) + 1)
     for copy in sides:
         copy.wait_recv()
     winf[0:subs] = recv0[0].astype(F32)
     winf[subs : 2 * subs] = unk_ref[...].astype(F32)
     winf[2 * subs : 3 * subs] = recv0[1].astype(F32)
-    relay(3)
     group_subs = subs * dirs
     sub_base = left * group_subs
 
@@ -337,6 +341,7 @@
         return carry
 
     lax.fori_loop(0, subs, couple, 0)
+
     for s in range(2, subs - 1):
         schur(s)
 
@@ -352,7 +357,7 @@
             b = first + k
             field = jnp.zeros((excites, directions), F32)
             for j in range(list_len):
-                field = field + trans_v[pl.ds(type_ref[j, b], 1), :] * patf[list_ref[j, b]]
+                field = field + trans_v[type_ref[j, b]] * patf[list_ref[j, b]]
             found.append(dot(field.astype(BF16), agg_v[b], 1, 0) + nearf[b])
         both = jnp.concatenate(found, axis=0).astype(BF16)
         size = pair * excites
@@ -438,7 +443,7 @@
     ]
     scratch = smem + [
         pltpu.VMEM((boxes, directions, slots), BF16),
-        pltpu.VMEM(trans_table.shape, F32),
+        pltpu.VMEM((trans_table.shape[0], excites, trans_table.shape[1]), F32),
         pltpu.VMEM(trans_table.shape[::-1], F32),
         pltpu.VMEM(row_map.shape, jnp.int32),
         pltpu.VMEM(coupling.shape, F32),

time: 32.1 us -> 31.7 us (0.988)
  Pallas kernels: 31.3 us -> 30.9 us
    pallas_call x1, Pallas kernels: 31.3 us -> 30.9 us  [shards(): pl.pallas_call(functools.partial(kernel, mesh_dims), out_shape=pltpu.VMEM...]
where the time goes in v5:
time: 31.7 us; the launch traced here: 31.6 us
  Pallas kernels  30.9 us (97%)
  local copies, waits for them, and re-layouts  0.66 us (2%)
    pallas_call x1, Pallas kernels, shards(): pl.pallas_call(functools.partial(kernel, mesh_dims), out_shape=pltpu.VMEM...  30.9 us
    unnamed x1, local copies, waits for them, and re-layouts  0.66 us

profile of v5, /device:TPU:0, one launch (start us, length us, event | category | flops | bytes accessed | tf_op | source)
XLA Modules:
  0.0 31.6 jit_solution(14108553932949105974)
XLA Ops:
  0.0 30.9 %shard_map.118 = f32[4,8,1024]{2,1,0:T(8,128)S(1)} custom-call(s32[4,4]{1,0:T(4,128)} %adj_hbm.1, s32[16,32]{1,0:T(8,128)} %bitcast.8, s32[16,32]{1,0:T(8,128)} %bitcast.9, s32[4,8]{1,0:T(4,128)} %bitcast.11, bf16[4,8,1024]{2,1,0:T(8,128)(2,1)} %unk_ref.1, s32[1,1024]{1,0:T(1,128)} %bitcast.10, bf16[32,288,256]{2,1,0:T(8,128)(2,1)} %bitcast.6, ...), custom_call_target="tpu_custom_call" | custom-call | tf_op jit(solution)/shard_map/pallas_call | solution.py:476
  30.9 0.7 %copy.14 = f32[4,8,1024]{2,1,0:T(8,128)} copy(f32[4,8,1024]{2,1,0:T(8,128)S(1)} %shard_map.118) | data formatting | bytes 262144

commit v6 on v5

--- a/solution.py
+++ b/solution.py
@@ -350,21 +350,23 @@
     for side, source in enumerate((partner, relay_source)):
         patf[pl.ds(source * boxes, boxes)] = recv2[side].astype(F32).reshape(boxes, excites, directions)
 
+    batch = 16
+
     def respond(i, carry):
-        first = i * pair
+        first = i * batch
         found = []
-        for k in range(pair):
+        for k in range(batch):
             b = first + k
             field = jnp.zeros((excites, directions), F32)
             for j in range(list_len):
                 field = field + trans_v[type_ref[j, b]] * patf[list_ref[j, b]]
             found.append(dot(field.astype(BF16), agg_v[b], 1, 0) + nearf[b])
         both = jnp.concatenate(found, axis=0).astype(BF16)
-        size = pair * excites
+        size = batch * excites
         total[pl.ds(pl.multiple_of(first * excites, size), size), :] = both
         return carry
 
-    lax.fori_loop(0, boxes // pair, respond, 0)
+    lax.fori_loop(0, boxes // batch, respond, 0)
     leaving = jnp.zeros((all_rows, LANES), F32)
     for h in range(halves):
         leaving = leaving + dot(perm[h], total[h * LANES : (h + 1) * LANES, :], 1, 1)

time: 31.7 us -> 31.4 us (level)
  no operation moved by 1% of the time
where the time goes in v6:
time: 31.4 us; the launch traced here: 31.3 us
  Pallas kernels  30.6 us (97%)
  local copies, waits for them, and re-layouts  0.66 us (2%)
    pallas_call x1, Pallas kernels, shards(): pl.pallas_call(functools.partial(kernel, mesh_dims), out_shape=pltpu.VMEM...  30.6 us
    unnamed x1, local copies, waits for them, and re-layouts  0.66 us

profile of v6, /device:TPU:0, one launch (start us, length us, event | category | flops | bytes accessed | tf_op | source)
XLA Modules:
  0.0 31.3 jit_solution(13856322346735277323)
XLA Ops:
  0.0 30.6 %shard_map.118 = f32[4,8,1024]{2,1,0:T(8,128)S(1)} custom-call(s32[4,4]{1,0:T(4,128)} %adj_hbm.1, s32[16,32]{1,0:T(8,128)} %bitcast.8, s32[16,32]{1,0:T(8,128)} %bitcast.9, s32[4,8]{1,0:T(4,128)} %bitcast.11, bf16[4,8,1024]{2,1,0:T(8,128)(2,1)} %unk_ref.1, s32[1,1024]{1,0:T(1,128)} %bitcast.10, bf16[32,288,256]{2,1,0:T(8,128)(2,1)} %bitcast.6, ...), custom_call_target="tpu_custom_call" | custom-call | tf_op jit(solution)/shard_map/pallas_call | solution.py:478
  30.6 0.7 %copy.14 = f32[4,8,1024]{2,1,0:T(8,128)} copy(f32[4,8,1024]{2,1,0:T(8,128)S(1)} %shard_map.118) | data formatting | bytes 262144
